TPU v7x, 256 devices: a whole 4x4x8 slice. The times are simulated.
256 devices in a mesh: group: 8 (over x, core), local: 32 (over z, y).
Axes of the slice: x: 4, y: 4, z: 8, core: 2. Of those that a mesh axis runs over, the one named last changes fastest.
Arguments:
- coords: float32 [3, 262144], P(None, ('group', 'local')), may hold values from -6 to 6
- inv_length: float32 [3], replicated, may hold values from 0.5 to 2
- noise: float32 [262144], P(('group', 'local')), may hold values from 1 to 4
- order: int32 [256, 1024], P(('group', 'local')), may hold values from 0 to 1023, each once within a row
- basis: bfloat16 [262144, 8, 256], P(('group', 'local')), may hold values from -6 to 6
- probes: float32 [128, 262144], P(None, ('group', 'local')), may hold values from -8 to 8
Outputs:
- solution: float32 [128, 262144], P(None, ('group', 'local'))
- residual: float32 [128, 262144], P(None, ('group', 'local'))
All inputs are finite; a program needn't handle non-finite values.
Results may differ from a plain program's by a relative error of at most 0.0003.
Values sent between devices are 32-bit elements; how exact they have to be, the bound alone decides.
No kernel may reach another device: no remote copies, remote signals or barrier semaphores. Data moves between devices by JAX's collectives and lax.ppermute only.
A program may use at most 64 MiB of HBM per device.

v0:
```python
import math

import jax
import jax.numpy as jnp
from jax import lax
from jax.sharding import PartitionSpec as P

ITERS = 2


GAMMA = 0.08
ROOT_OF_THREE = math.sqrt(3.0)


def partner_2(x, axis, bit):
    return lax.ppermute(x, axis, [(i, i ^ 1 << bit) for i in range(lax.axis_size(axis))])


def leaf_kernel(input_locations, inv_length):
    scaled_distance = input_locations * inv_length[:, None]
    square = jnp.zeros((input_locations.shape[1], input_locations.shape[1]), jnp.float32)
    for comp in range(3):
        diff = scaled_distance[comp][:, None] - scaled_distance[comp][None, :]
        square = square + diff * diff
    dist = jnp.sqrt(square)
    return (1.0 + ROOT_OF_THREE * dist) * jnp.exp(-ROOT_OF_THREE * dist)


def distant_contribution(vector, basis):
    input_locations = basis.shape[0]
    levels = basis.shape[1]
    rank = basis.shape[2]
    fine = lax.axis_size("local").bit_length() - 1
    flat = basis.reshape(input_locations, levels * rank)
    rounded_values = vector.astype(jnp.bfloat16)
    terms = jnp.dot(rounded_values, flat, preferred_element_type=jnp.float32).reshape(
        -1, levels, rank
    )
    siblings = []
    upper = terms
    for bit in range(fine):
        partner = partner_2(upper, "local", bit)
        siblings.append(partner[:, 0])
        upper = upper[:, 1:] + partner[:, 1:]
    for bit in range(levels - fine):
        partner = partner_2(upper, "group", bit)
        siblings.append(partner[:, 0])
        upper = upper[:, 1:] + partner[:, 1:]
    factors = jnp.asarray(
        [GAMMA / (input_locations * 2.0**level) for level in range(levels)], jnp.float32
    )
    coeffs = (jnp.stack(siblings, axis=1) * factors[None, :, None]).astype(jnp.bfloat16)
    coeffs = coeffs.reshape(-1, levels * rank)
    return lax.dot_general(
        coeffs, flat, (((1,), (1,)), ((), ())), preferred_element_type=jnp.float32
    )


def squares(residual):
    return lax.psum(jnp.sum(residual * residual, axis=1), ("group", "local"))


def per_device(coords, inv_length, noise, order, basis, probes):
    index = order[0]
    tree_coords = jnp.take(coords, index, axis=1)
    tree_noise = jnp.take(noise, index, axis=0)
    solution = jnp.zeros_like(probes)
    residual = probes
    direction = probes
    norm_now = squares(residual)
    for step in range(ITERS):
        kernel = leaf_kernel(tree_coords, inv_length)
        near = (
            jnp.dot(direction, kernel, precision=lax.Precision.HIGHEST)
            + tree_noise[None, :] * direction
        )
        image = near + distant_contribution(direction, basis)
        curve = lax.psum(jnp.sum(direction * image, axis=1), ("group", "local"))
        alpha = norm_now / curve
        solution = solution + alpha[:, None] * direction
        residual = residual - alpha[:, None] * image
        norm_next = squares(residual)
        direction = residual + (norm_next / norm_now)[:, None] * direction
        norm_now = norm_next
    return (solution, residual)


def solution(mesh):
    in_specs = (
        P(None, ("group", "local")),
        P(),
        P(("group", "local")),
        P(("group", "local"), None),
        P(("group", "local"), None, None),
        P(None, ("group", "local")),
    )
    out_specs = (P(None, ("group", "local")), P(None, ("group", "local")))
    return jax.shard_map(
        per_device, mesh=mesh, in_specs=in_specs, out_specs=out_specs, check_vma=False
    )
```

profile of v0, /device:TPU:1, one launch (start us, length us, event | category | flops | bytes accessed | tf_op | source)
XLA Modules:
  0.0 537.7 jit_solution(18283998542749825333)
XLA Ops:
  0.6 5.6 %copy.47 = bf16[128,8,8,256]{3,1,2,0:T(8,128)(2,1)} copy(bf16[128,8,8,256]{3,2,1,0:T(8,128)(2,1)} %bitcast.35) | data formatting | bytes 8388608
  6.3 6.5 %copy.27 = bf16[2048,1024]{1,0:T(8,128)(2,1)} copy(bf16[2048,1024]{0,1:T(8,128)(2,1)} %bitcast.38) | data formatting | bytes 8388608 | tf_op jit(solution)/shard_map/dot_general | solution.py:36
  18.7 21.6 %collective-permute-done = f32[128,8,256]{2,0,1:T(8,128)S(1)} collective-permute-done((f32[128,8,256]{2,0,1:T(8,128)S(1)}, f32[128,8,256]{2,0,1:T(8,128)S(1)}, u32[]{:S(2)}, u32[]{:S(2)}) %collective-permute-start) | collective-permute-done | bytes 1048608 | tf_op jit(solution)/shard_map/ppermute | solution.py:16
  40.5 4.1 collective-permute-start.1
  44.6 19.0 %collective-permute-done.1 = f32[128,7,256]{2,0,1:T(8,128)S(1)} collective-permute-done((f32[128,7,256]{2,0,1:T(8,128)S(1)}, f32[128,7,256]{2,0,1:T(8,128)S(1)}, u32[]{:S(2)}, u32[]{:S(2)}) %collective-permute-start.1) | collective-permute-done | bytes 917536 | tf_op jit(solution)/shard_map/ppermute | solution.py:16
  65.3 15.3 %collective-permute-done.2 = f32[128,6,256]{2,0,1:T(8,128)S(1)} collective-permute-done((f32[128,6,256]{2,0,1:T(8,128)S(1)}, f32[128,6,256]{2,0,1:T(8,128)S(1)}, u32[]{:S(2)}, u32[]{:S(2)}) %collective-permute-start.2) | collective-permute-done | bytes 786464 | tf_op jit(solution)/shard_map/ppermute | solution.py:16
  84.2 4.5 gather_fusion.1
  88.7 4.0 gather_fusion
  94.8 17.1 %collective-permute-done.3 = f32[128,5,256]{2,0,1:T(8,128)} collective-permute-done((f32[128,5,256]{2,0,1:T(8,128)S(1)}, f32[128,5,256]{2,0,1:T(8,128)}, u32[]{:S(2)}, u32[]{:S(2)}) %collective-permute-start.3) | collective-permute-done | bytes 655392 | tf_op jit(solution)/shard_map/ppermute | solution.py:16
  113.0 7.2 %collective-permute-start.4 = (f32[128,4,256]{2,0,1:T(8,128)S(1)}, f32[128,4,256]{2,0,1:T(8,128)S(1)}, u32[]{:S(2)}, u32[]{:S(2)}) collective-permute-start(f32[128,4,256]{2,0,1:T(8,128)S(1)} %slice_add_fusion.7), channel_id=1, source_target_pairs={{0,16},{1,17},{2,18},{3,19},{4,20},{5,21},{6,22},{7,23},{8,24},{9,... | collective-permute-start | bytes 1572872 | tf_op jit(solution)/shard_map/ppermute | solution.py:16
  120.2 9.3 %fusion.37 = f32[128,1024]{0,1:T(8,128)S(1)} fusion(f32[128,1024]{1,0:T(8,128)S(1)} %copy-done.3, f32[1024]{0:T(1024)S(1)} %get-tuple-element.7, f32[1024]{0:T(1024)S(1)} %get-tuple-element.8, f32[1024]{0:T(1024)S(1)} %get-tuple-element.6, f32[128,1024]{0,1:T(8,128)S(1)} %copy.30, f32[1024]{0:T(1024)S(1)} %bitcast.42), kind=kOutput, calls=%fused_computation.32 | convolution fusion | flops 1623457792 | bytes 1589248 | tf_op jit(solution)/shard_map/dot_general | solution.py:74
  130.6 12.2 %collective-permute-done.4 = f32[128,4,256]{2,0,1:T(8,128)S(1)} collective-permute-done((f32[128,4,256]{2,0,1:T(8,128)S(1)}, f32[128,4,256]{2,0,1:T(8,128)S(1)}, u32[]{:S(2)}, u32[]{:S(2)}) %collective-permute-start.4) | collective-permute-done | bytes 524320 | tf_op jit(solution)/shard_map/ppermute | solution.py:16
  147.9 6.7 %collective-permute-done.6 = f32[128,2,256]{2,0,1:T(8,128)S(1)} collective-permute-done((f32[128,2,256]{2,0,1:T(8,128)S(1)}, f32[128,2,256]{2,0,1:T(8,128)S(1)}, u32[]{:S(2)}, u32[]{:S(2)}) %collective-permute-start.6) | collective-permute-done | bytes 262176 | tf_op jit(solution)/shard_map/ppermute | solution.py:16
  161.9 77.2 %all-reduce = (f32[128]{0:T(128)S(1)}, f32[128]{0:T(128)S(1)}) all-reduce(f32[128]{0:T(128)S(1)} %multiply_reduce_fusion.3, f32[128]{0:T(128)S(1)} %get-tuple-element.17), channel_id=1, replica_groups=mesh['group'=8,'local'=32] {'group','local'}, use_global_device_ids=true, to_apply=%region_1.2 | all-reduce | flops 256 | bytes 2048 | tf_op jit(solution)/shard_map/psum | solution.py:60
  239.3 72.7 %psum.30 = f32[128]{0:T(128)S(1)} all-reduce(f32[128]{0:T(128)S(1)} %multiply_reduce_fusion.1), channel_id=1, replica_groups=mesh['group'=8,'local'=32] {'group','local'}, use_global_device_ids=true, to_apply=%region_5.6 | all-reduce | flops 128 | bytes 1024 | tf_op jit(solution)/shard_map/psum | solution.py:60
  312.1 3.7 fusion.41
  316.6 23.3 %collective-permute-done.8 = f32[128,8,256]{2,0,1:T(8,128)S(1)} collective-permute-done((f32[128,8,256]{2,0,1:T(8,128)S(1)}, f32[128,8,256]{2,0,1:T(8,128)S(1)}, u32[]{:S(2)}, u32[]{:S(2)}) %collective-permute-start.8) | collective-permute-done | bytes 1048608 | tf_op jit(solution)/shard_map/ppermute | solution.py:16
  342.1 19.8 %collective-permute-done.9 = f32[128,7,256]{2,0,1:T(8,128)S(1)} collective-permute-done((f32[128,7,256]{2,0,1:T(8,128)S(1)}, f32[128,7,256]{2,0,1:T(8,128)S(1)}, u32[]{:S(2)}, u32[]{:S(2)}) %collective-permute-start.9) | collective-permute-done | bytes 917536 | tf_op jit(solution)/shard_map/ppermute | solution.py:16
  363.9 15.4 %collective-permute-done.10 = f32[128,6,256]{2,0,1:T(8,128)S(1)} collective-permute-done((f32[128,6,256]{2,0,1:T(8,128)S(1)}, f32[128,6,256]{2,0,1:T(8,128)S(1)}, u32[]{:S(2)}, u32[]{:S(2)}) %collective-permute-start.10) | collective-permute-done | bytes 786464 | tf_op jit(solution)/shard_map/ppermute | solution.py:16
  380.6 29.5 %collective-permute-done.11 = f32[128,5,256]{2,0,1:T(8,128)S(1)} collective-permute-done((f32[128,5,256]{2,0,1:T(8,128)S(1)}, f32[128,5,256]{2,0,1:T(8,128)S(1)}, u32[]{:S(2)}, u32[]{:S(2)}) %collective-permute-start.11) | collective-permute-done | bytes 655392 | tf_op jit(solution)/shard_map/ppermute | solution.py:16
  413.5 25.6 %collective-permute-done.12 = f32[128,4,256]{2,0,1:T(8,128)S(1)} collective-permute-done((f32[128,4,256]{2,0,1:T(8,128)S(1)}, f32[128,4,256]{2,0,1:T(8,128)S(1)}, u32[]{:S(2)}, u32[]{:S(2)}) %collective-permute-start.12) | collective-permute-done | bytes 524320 | tf_op jit(solution)/shard_map/ppermute | solution.py:16
  442.1 6.7 %collective-permute-done.14 = f32[128,2,256]{2,0,1:T(8,128)S(1)} collective-permute-done((f32[128,2,256]{2,0,1:T(8,128)S(1)}, f32[128,2,256]{2,0,1:T(8,128)S(1)}, u32[]{:S(2)}, u32[]{:S(2)}) %collective-permute-start.14) | collective-permute-done | bytes 262176 | tf_op jit(solution)/shard_map/ppermute | solution.py:16
  451.2 8.9 %fusion.38 = f32[128,1024]{0,1:T(8,128)S(1)} fusion(f32[128,1024]{0,1:T(8,128)S(1)} %multiply_add_fusion.1, f32[1024]{0:T(1024)S(1)} %get-tuple-element.7, f32[1024]{0:T(1024)S(1)} %get-tuple-element.8, f32[1024]{0:T(1024)S(1)} %get-tuple-element.6, f32[1024]{0:T(1024)S(1)} %bitcast.43), kind=kOutput, calls=%fused_computation.33 | convolution fusion | flops 1623457792 | bytes 1064960 | tf_op jit(solution)/shard_map/dot_general | solution.py:74
  461.5 73.8 %psum.31 = f32[128]{0:T(128)S(1)} all-reduce(f32[128]{0:T(128)S(1)} %get-tuple-element.19), channel_id=1, replica_groups=mesh['group'=8,'local'=32] {'group','local'}, use_global_device_ids=true, to_apply=%region_7.8 | all-reduce | flops 128 | bytes 1024 | tf_op jit(solution)/shard_map/psum | solution.py:78
  (86 shorter events, 46.7 us)
Async XLA Ops:
  0.6 83.5 %copy-start = (f32[1024]{0:T(1024)S(1)}, f32[1024]{0:T(1024)}, u32[]{:S(2)}) copy-start(f32[1024]{0:T(1024)} %param.10) | copy-start | bytes 12292
  12.8 52.5 %copy-start.6 = (s32[1,1024]{1,0:T(1,128)S(1)}, s32[1,1024]{1,0:T(1,128)}, u32[]{:S(2)}) copy-start(s32[1,1024]{1,0:T(1,128)} %param.11) | copy-start | bytes 12292
  16.5 67.4 %copy-start.7 = (f32[3,1024]{1,0:T(4,128)S(1)}, f32[3,1024]{1,0:T(4,128)}, u32[]{:S(2)}) copy-start(f32[3,1024]{1,0:T(4,128)} %param.8) | copy-start | bytes 36868
  16.5 23.8 %collective-permute-start = (f32[128,8,256]{2,0,1:T(8,128)S(1)}, f32[128,8,256]{2,0,1:T(8,128)S(1)}, u32[]{:S(2)}, u32[]{:S(2)}) collective-permute-start(f32[128,8,256]{2,0,1:T(8,128)S(1)} %fusion.43), channel_id=1, source_target_pairs={{0,1},{1,0},{2,3},{3,2},{4,5},{5,4},{6,7},{7,6},{8,9},{9,8},{10,11... | collective-permute-start | bytes 3145736 | tf_op jit(solution)/shard_map/ppermute | solution.py:16
  40.5 23.1 %collective-permute-start.1 = (f32[128,7,256]{2,0,1:T(8,128)S(1)}, f32[128,7,256]{2,0,1:T(8,128)S(1)}, u32[]{:S(2)}, u32[]{:S(2)}) collective-permute-start(f32[128,7,256]{2,0,1:T(8,128)S(1)} %slice_add_fusion.1), channel_id=1, source_target_pairs={{0,2},{1,3},{2,0},{3,1},{4,6},{5,7},{6,4},{7,5},{8,10},{9,11},{10,... | collective-permute-start | bytes 2752520 | tf_op jit(solution)/shard_map/ppermute | solution.py:16
  63.5 20.2 %copy-start.4 = (f32[128,7,256]{2,0,1:T(8,128)}, f32[128,7,256]{2,0,1:T(8,128)S(1)}, u32[]{:S(2)}) copy-start(f32[128,7,256]{2,0,1:T(8,128)S(1)} %collective-permute-done.1) | copy-start | bytes 2752516
  63.6 29.1 %copy-start.9 = (f32[3]{0:T(128)S(1)}, f32[3]{0:T(128)}, u32[]{:S(2)}) copy-start(f32[3]{0:T(128)} %param.9) | copy-start | bytes 40
  63.6 17.0 %collective-permute-start.2 = (f32[128,6,256]{2,0,1:T(8,128)S(1)}, f32[128,6,256]{2,0,1:T(8,128)S(1)}, u32[]{:S(2)}, u32[]{:S(2)}) collective-permute-start(f32[128,6,256]{2,0,1:T(8,128)S(1)} %slice_add_fusion.3), channel_id=1, source_target_pairs={{0,4},{1,5},{2,6},{3,7},{4,0},{5,1},{6,2},{7,3},{8,12},{9,13},{10,... | collective-permute-start | bytes 2359304 | tf_op jit(solution)/shard_map/ppermute | solution.py:16
  80.7 31.1 %collective-permute-start.3 = (f32[128,5,256]{2,0,1:T(8,128)S(1)}, f32[128,5,256]{2,0,1:T(8,128)}, u32[]{:S(2)}, u32[]{:S(2)}) collective-permute-start(f32[128,5,256]{2,0,1:T(8,128)S(1)} %slice_add_fusion.5), channel_id=1, source_target_pairs={{0,8},{1,9},{2,10},{3,11},{4,12},{5,13},{6,14},{7,15},{8,0},{9,1},... | collective-permute-start | bytes 1966088 | tf_op jit(solution)/shard_map/ppermute | solution.py:16
  113.0 29.8 %collective-permute-start.4 = (f32[128,4,256]{2,0,1:T(8,128)S(1)}, f32[128,4,256]{2,0,1:T(8,128)S(1)}, u32[]{:S(2)}, u32[]{:S(2)}) collective-permute-start(f32[128,4,256]{2,0,1:T(8,128)S(1)} %slice_add_fusion.7), channel_id=1, source_target_pairs={{0,16},{1,17},{2,18},{3,19},{4,20},{5,21},{6,22},{7,23},{8,24},{9,... | collective-permute-start | bytes 1572872 | tf_op jit(solution)/shard_map/ppermute | solution.py:16
  129.5 31.1 %copy-start.1 = (bf16[1024,8,256]{2,1,0:T(8,128)(2,1)S(1)}, bf16[1024,8,256]{2,1,0:T(8,128)(2,1)}, u32[]{:S(2)}) copy-start(bf16[1024,8,256]{2,1,0:T(8,128)(2,1)} %param.12) | copy-start | bytes 12582916
  129.5 31.1 %copy-start.8 = (f32[8]{0:T(128)S(1)}, f32[8]{0:T(128)}, u32[]{:S(2)}) copy-start(f32[8]{0:T(128)} %constant.38.clone) | copy-start | bytes 100
  142.9 3.6 collective-permute-start.5
  146.5 8.0 %collective-permute-start.6 = (f32[128,2,256]{2,0,1:T(8,128)S(1)}, f32[128,2,256]{2,0,1:T(8,128)S(1)}, u32[]{:S(2)}, u32[]{:S(2)}) collective-permute-start(f32[128,2,256]{2,0,1:T(8,128)S(1)} %slice_add_fusion.11), channel_id=1, source_target_pairs={{0,64},{32,96},{64,0},{96,32},{128,192},{160,224},{192,128},{224,1... | collective-permute-start | bytes 786440 | tf_op jit(solution)/shard_map/ppermute | solution.py:16
  154.5 6.0 %collective-permute-start.7 = (f32[128,1,256]{2,0,1:T(8,128)S(1)}, f32[128,1,256]{2,0,1:T(8,128)S(1)}, u32[]{:S(2)}, u32[]{:S(2)}) collective-permute-start(f32[128,1,256]{2,0,1:T(8,128)S(1)} %get-tuple-element.15), channel_id=1, source_target_pairs={{0,128},{32,160},{64,192},{96,224},{128,0},{160,32},{192,64},{224,... | collective-permute-start | bytes 393224 | tf_op jit(solution)/shard_map/ppermute | solution.py:16
  315.8 24.1 %collective-permute-start.8 = (f32[128,8,256]{2,0,1:T(8,128)S(1)}, f32[128,8,256]{2,0,1:T(8,128)S(1)}, u32[]{:S(2)}, u32[]{:S(2)}) collective-permute-start(f32[128,8,256]{2,0,1:T(8,128)S(1)} %fusion.41), channel_id=1, source_target_pairs={{0,1},{1,0},{2,3},{3,2},{4,5},{5,4},{6,7},{7,6},{8,9},{9,8},{10,11... | collective-permute-start | bytes 3145736 | tf_op jit(solution)/shard_map/ppermute | solution.py:16
  340.0 21.9 %collective-permute-start.9 = (f32[128,7,256]{2,0,1:T(8,128)S(1)}, f32[128,7,256]{2,0,1:T(8,128)S(1)}, u32[]{:S(2)}, u32[]{:S(2)}) collective-permute-start(f32[128,7,256]{2,0,1:T(8,128)S(1)} %slice_add_fusion), channel_id=1, source_target_pairs={{0,2},{1,3},{2,0},{3,1},{4,6},{5,7},{6,4},{7,5},{8,10},{9,11},{10,... | collective-permute-start | bytes 2752520 | tf_op jit(solution)/shard_map/ppermute | solution.py:16
  362.0 17.2 %collective-permute-start.10 = (f32[128,6,256]{2,0,1:T(8,128)S(1)}, f32[128,6,256]{2,0,1:T(8,128)S(1)}, u32[]{:S(2)}, u32[]{:S(2)}) collective-permute-start(f32[128,6,256]{2,0,1:T(8,128)S(1)} %slice_add_fusion.2), channel_id=1, source_target_pairs={{0,4},{1,5},{2,6},{3,7},{4,0},{5,1},{6,2},{7,3},{8,12},{9,13},{10,... | collective-permute-start | bytes 2359304 | tf_op jit(solution)/shard_map/ppermute | solution.py:16
  379.4 30.7 %collective-permute-start.11 = (f32[128,5,256]{2,0,1:T(8,128)S(1)}, f32[128,5,256]{2,0,1:T(8,128)S(1)}, u32[]{:S(2)}, u32[]{:S(2)}) collective-permute-start(f32[128,5,256]{2,0,1:T(8,128)S(1)} %slice_add_fusion.4), channel_id=1, source_target_pairs={{0,8},{1,9},{2,10},{3,11},{4,12},{5,13},{6,14},{7,15},{8,0},{9,1},... | collective-permute-start | bytes 1966088 | tf_op jit(solution)/shard_map/ppermute | solution.py:16
  410.2 29.0 %collective-permute-start.12 = (f32[128,4,256]{2,0,1:T(8,128)S(1)}, f32[128,4,256]{2,0,1:T(8,128)S(1)}, u32[]{:S(2)}, u32[]{:S(2)}) collective-permute-start(f32[128,4,256]{2,0,1:T(8,128)S(1)} %slice_add_fusion.6), channel_id=1, source_target_pairs={{0,16},{1,17},{2,18},{3,19},{4,20},{5,21},{6,22},{7,23},{8,24},{9,... | collective-permute-start | bytes 1572872 | tf_op jit(solution)/shard_map/ppermute | solution.py:16
  439.2 2.0 collective-permute-start.13
  441.2 7.6 %collective-permute-start.14 = (f32[128,2,256]{2,0,1:T(8,128)S(1)}, f32[128,2,256]{2,0,1:T(8,128)S(1)}, u32[]{:S(2)}, u32[]{:S(2)}) collective-permute-start(f32[128,2,256]{2,0,1:T(8,128)S(1)} %slice_add_fusion.10), channel_id=1, source_target_pairs={{0,64},{32,96},{64,0},{96,32},{128,192},{160,224},{192,128},{224,1... | collective-permute-start | bytes 786440 | tf_op jit(solution)/shard_map/ppermute | solution.py:16
  448.9 11.2 %copy-start.2 = (bf16[1024,8,256]{2,1,0:T(8,128)(2,1)S(1)}, bf16[1024,8,256]{2,1,0:T(8,128)(2,1)}, u32[]{:S(2)}) copy-start(bf16[1024,8,256]{2,1,0:T(8,128)(2,1)} %param.12) | copy-start | bytes 12582916
  448.9 11.2 %collective-permute-start.15 = (f32[128,1,256]{2,0,1:T(8,128)S(1)}, f32[128,1,256]{2,0,1:T(8,128)S(1)}, u32[]{:S(2)}, u32[]{:S(2)}) collective-permute-start(f32[128,1,256]{2,0,1:T(8,128)S(1)} %get-tuple-element.13), channel_id=1, source_target_pairs={{0,128},{32,160},{64,192},{96,224},{128,0},{160,32},{192,64},{224,... | collective-permute-start | bytes 393224 | tf_op jit(solution)/shard_map/ppermute | solution.py:16
  (2 other events, 9.5 us)
where the time goes:
time: 544 us; the launch traced here: 538 us
  blocking collectives  224 us (41%)
  waiting for transfers between devices  216 us (40%)
  starting transfers between devices  37.3 us (7%)
  matrix products  28.3 us (5%)
  local copies, waits for them, and re-layouts  26.9 us (5%)
    ppermute x16, waiting for transfers between devices, partner_2(): lax.ppermute(x, axis, [(i, i ^ 1 << bit) for i in range(lax.axis_size(axi...  216 us
    psum x2, blocking collectives, squares(): return lax.psum(jnp.sum(residual * residual, axis=1), ('group', 'local'))  150 us
    psum x1, blocking collectives, per_device(): curve = lax.psum(jnp.sum(direction * image, axis=1), ('group', 'local'))  73.8 us
    ppermute x16, starting transfers between devices, partner_2(): lax.ppermute(x, axis, [(i, i ^ 1 << bit) for i in range(lax.axis_size(axi...  37.3 us
    dot_general x2, matrix products, per_device(): jnp.dot(direction, kernel, precision=lax.Precision.HIGHEST)  18.2 us
    unnamed x37, local copies, waits for them, and re-layouts  11.1 us
  transfers between devices with their start and end apart: 16, of which 14 were waited for; matrix products, arithmetic and copies ran while one was open for 6% of the time, Pallas kernels for 0%

commit v1 on v0

v1 whole, which is shorter than its diff:
```python
import functools
import math

import jax
import jax.numpy as jnp
from jax import lax
from jax.experimental import pallas as pl
from jax.experimental.pallas import tpu as pltpu
from jax.sharding import PartitionSpec as P

GAMMA = 0.08
ROOT_OF_THREE = math.sqrt(3.0)
LEVELS = 8
RANK = 256
LEAF = 1024
PROBES = 128
PART = PROBES // 4
LANES = 128
F32 = jnp.float32
BF16 = jnp.bfloat16
VMEM_LIMIT = 48 * 2**20


def factor(level):
    return GAMMA / (LEAF * 2.0**level)


def call(kernel, out_shape, *args, scratch=(), smem=0, flops=0):
    specs = [pl.BlockSpec(memory_space=pltpu.SMEM)] * smem
    specs += [pl.BlockSpec(memory_space=pltpu.VMEM)] * (len(args) - smem)
    return pl.pallas_call(
        kernel,
        out_shape=out_shape,
        in_specs=specs,
        out_specs=jax.tree.map(
            lambda _: pl.BlockSpec(memory_space=pltpu.VMEM), out_shape
        ),
        scratch_shapes=list(scratch),
        compiler_params=pltpu.CompilerParams(vmem_limit_bytes=VMEM_LIMIT),
        cost_estimate=pl.CostEstimate(
            flops=flops, bytes_accessed=2**20, transcendentals=0
        ),
    )(*args)


def shape(*dims, dtype=F32):
    return jax.ShapeDtypeStruct(dims, dtype)


def dot(a, b):
    return jnp.dot(a, b, preferred_element_type=F32)


def dot_t(a, b):
    return lax.dot_general(a, b, (((1,), (1,)), ((), ())), preferred_element_type=F32)


def split(x):
    high = x.astype(BF16)
    return high, (x - high.astype(F32)).astype(BF16)


def near_product(v, high_ref, low_ref):
    v_high, v_low = split(v)
    return (
        dot(v_low, high_ref[...]) + dot(v_high, low_ref[...]) + dot(v_high, high_ref[...])
    )


def hand_out(y, full_ref, part_refs):
    for k, part_ref in enumerate(part_refs):
        part_ref[...] = full_ref[pl.ds(pl.multiple_of((y ^ k) * PART, PART), PART), :]


def coefficients_kernel(y_ref, v_ref, basis_ref, *rest):
    parts, full = rest[:4], rest[4]
    v = v_ref[...].astype(BF16)
    for level in range(LEVELS):
        full[:, level * RANK : (level + 1) * RANK] = dot(v, basis_ref[level])
    hand_out(y_ref[0], full, parts)


def kernel_matrix_kernel(rows_ref, cols_ref, noise_ref, v_ref, near_ref, high_ref, low_ref):
    step = 128

    @pl.loop(0, LEAF // step)
    def _(i):
        at = pl.ds(pl.multiple_of(i * step, step), step)
        square = jnp.zeros((step, LEAF), F32)
        for c in range(3):
            diff = cols_ref[at, c : c + 1] - rows_ref[c : c + 1, :]
            square = square + diff * diff
        t = ROOT_OF_THREE * jnp.sqrt(square)
        value = (1.0 + t) * jnp.exp(-t)
        high, low = split(value)
        high_ref[at, :] = high
        low_ref[at, :] = low

    v = v_ref[...]
    near_ref[...] = near_product(v, high_ref, low_ref) + noise_ref[...] * v


def gather_far(y, back_refs, sib_ref, basis_ref):
    for k, back_ref in enumerate(back_refs):
        at = pl.ds(pl.multiple_of((y ^ k) * PART, PART), PART)
        for level in range(LEVELS):
            lanes = slice(level * RANK, (level + 1) * RANK)
            sib_ref[at, lanes] = (back_ref[:, lanes] * factor(level)).astype(BF16)
    far = dot_t(sib_ref[:, :RANK], basis_ref[0])
    for level in range(1, LEVELS):
        far += dot_t(sib_ref[:, level * RANK : (level + 1) * RANK], basis_ref[level])
    return far


def image_kernel(y_ref, *refs):
    backs = refs[:4]
    basis_ref, near_ref, v_ref, high_ref, low_ref, noise_ref = refs[4:10]
    parts = refs[10:14]
    image_ref, next_near_ref, sib_ref, full = refs[14:]
    y = y_ref[0]
    image = near_ref[...] + gather_far(y, backs, sib_ref, basis_ref)
    image_ref[...] = image
    rounded = image.astype(BF16)
    for level in range(LEVELS):
        full[:, level * RANK : (level + 1) * RANK] = dot(rounded, basis_ref[level])
    next_near = near_product(image, high_ref, low_ref) + noise_ref[...] * image
    next_near_ref[...] = next_near
    v = v_ref[...]
    lane = lax.broadcasted_iota(jnp.int32, (PROBES, LANES), 1)
    block = jnp.zeros((PROBES, LANES), F32)
    for i, term in enumerate((v * v, v * image, image * image, image * next_near)):
        block = jnp.where(lane == i, jnp.sum(term, axis=1, keepdims=True), block)
    full[:, LEVELS * RANK :] = block
    hand_out(y, full, parts)


def final_kernel(y_ref, *refs):
    backs = refs[:4]
    basis_ref, near_ref, image_ref, v_ref, x_ref, r_ref, sib_ref, dots = refs[4:]
    y = y_ref[0]
    for k, back_ref in enumerate(backs):
        at = pl.ds(pl.multiple_of((y ^ k) * PART, PART), PART)
        dots[at, :] = back_ref[:, LEVELS * RANK :]
    second = near_ref[...] + gather_far(y, backs, sib_ref, basis_ref)
    m0, m1, m2, m3 = (dots[:, i : i + 1] for i in range(4))
    alpha = m0 / m1
    ratio = m2 / m1
    norm = alpha * alpha * m2 - m0
    curve = alpha * alpha * (m3 - ratio * m2)
    alpha_next = norm / curve
    grown = alpha * ratio
    v = v_ref[...]
    image = image_ref[...]
    x_ref[...] = alpha * v + alpha_next * (grown * v - alpha * image)
    r_ref[...] = v - alpha * image - alpha_next * (grown * image - alpha * second)


def pair_dot(a, b, level):
    return 2.0 * factor(level) * jnp.sum(a * b, axis=1, keepdims=True)


def third(x):
    lane = lax.broadcasted_iota(jnp.int32, (PART, LANES), 1)
    return jnp.where(lane == 3, x, 0.0)


def low_kernel(dots, r0, r1, r2, r3, total_ref):
    start = 2 * RANK
    total_ref[...] = (r0[:, start:] + r1[:, start:]) + (r2[:, start:] + r3[:, start:])
    if dots:
        a, b = slice(0, RANK), slice(RANK, 2 * RANK)
        term = pair_dot(r0[:, a], r1[:, a], 0) + pair_dot(r2[:, a], r3[:, a], 0)
        term += pair_dot(r0[:, b] + r1[:, b], r2[:, b] + r3[:, b], 1)
        total_ref[:, -LANES:] += third(term)


def step_kernel(dots, level, own, other, total_ref):
    total_ref[...] = own[:, RANK:] + other[:, RANK:]
    if dots:
        total_ref[:, -LANES:] += third(pair_dot(own[:, :RANK], other[:, :RANK], level))


def back_kernel(dots, *refs):
    r, sibs = refs[:4], refs[4:10]
    outs = refs[10:] if not dots else refs[11:]
    for k in range(4):
        outs[k][:, :RANK] = r[k ^ 1][:, :RANK]
        outs[k][:, RANK : 2 * RANK] = (
            r[k ^ 2][:, RANK : 2 * RANK] + r[k ^ 3][:, RANK : 2 * RANK]
        )
        for level in range(2, LEVELS):
            lanes = slice(level * RANK, (level + 1) * RANK)
            outs[k][:, lanes] = sibs[level - 2][:, :RANK]
        if dots:
            outs[k][:, LEVELS * RANK :] = refs[10][...]


def swap(x, axis, mask):
    return lax.ppermute(x, axis, [(i, i ^ mask) for i in range(lax.axis_size(axis))])


HOPS = (("local", 4), ("local", 8), ("local", 24), ("group", 1), ("group", 2), ("group", 6))


def exchange(parts, dots):
    extra = LANES if dots else 0
    moved = [parts[0]] + [swap(parts[k], "local", k) for k in (1, 2, 3)]
    total = call(
        functools.partial(low_kernel, dots),
        shape(PART, (LEVELS - 2) * RANK + extra),
        *moved,
    )
    sibs = []
    for level, (axis, mask) in enumerate(HOPS, 2):
        other = swap(total, axis, mask)
        sibs.append(other)
        width = (LEVELS - 1 - level) * RANK + extra
        if width:
            total = call(
                functools.partial(step_kernel, dots, level),
                shape(PART, width),
                total,
                other,
            )
    outs = call(
        functools.partial(back_kernel, dots),
        (shape(PART, LEVELS * RANK + extra),) * 4,
        *moved,
        *sibs,
        *([total] if dots else []),
    )
    return [outs[0]] + [swap(outs[k], "local", k) for k in (1, 2, 3)]


def per_device(coords, inv_length, noise, order, basis, probes):
    index = order[0]
    scaled = jnp.take(coords, index, axis=1) * inv_length[:, None]
    tree_noise = jnp.take(noise, index, axis=0)[None, :]
    y = (lax.axis_index("local") & 3).astype(jnp.int32)[None]
    levels_first = jnp.transpose(basis, (1, 0, 2))
    full = LEVELS * RANK
    parts = call(
        coefficients_kernel,
        (shape(PART, full),) * 4,
        y,
        probes,
        levels_first,
        scratch=[pltpu.VMEM((PROBES, full), F32)],
        smem=1,
        flops=2 * PROBES * LEAF * full,
    )
    square = shape(LEAF, LEAF, dtype=BF16)
    vectors = shape(PROBES, LEAF)
    near, high, low = call(
        kernel_matrix_kernel,
        (vectors, square, square),
        scaled,
        scaled.T,
        tree_noise,
        probes,
        flops=6 * PROBES * LEAF * LEAF,
    )
    backs = exchange(parts, False)
    *parts, image, near = call(
        image_kernel,
        (shape(PART, full + LANES),) * 4 + (vectors, vectors),
        y,
        *backs,
        levels_first,
        near,
        probes,
        high,
        low,
        tree_noise,
        scratch=[pltpu.VMEM((PROBES, full), BF16), pltpu.VMEM((PROBES, full + LANES), F32)],
        smem=1,
        flops=4 * PROBES * LEAF * full,
    )
    backs = exchange(parts, True)
    return call(
        final_kernel,
        (vectors, vectors),
        y,
        *backs,
        levels_first,
        near,
        image,
        probes,
        scratch=[pltpu.VMEM((PROBES, full), BF16), pltpu.VMEM((PROBES, LANES), F32)],
        smem=1,
        flops=2 * PROBES * LEAF * full,
    )


def solution(mesh):
    in_specs = (
        P(None, ("group", "local")),
        P(),
        P(("group", "local")),
        P(("group", "local"), None),
        P(("group", "local"), None, None),
        P(None, ("group", "local")),
    )
    out_specs = (P(None, ("group", "local")), P(None, ("group", "local")))
    return jax.shard_map(
        per_device, mesh=mesh, in_specs=in_specs, out_specs=out_specs, check_vma=False
    )
```

time: 544 us -> 161 us (0.30); the launches traced: 538 us -> 160 us
  blocking collectives: 224 us -> 0 us
  waiting for transfers between devices: 216 us -> 76.7 us
  matrix products: 28.3 us -> 0 us
  Pallas kernels: 0 us -> 18 us
  local copies, waits for them, and re-layouts: 26.9 us -> 17.8 us
  starting transfers between devices: 37.3 us -> 45.5 us
    psum x3 -> x0, blocking collectives: 224 us -> none  [the longest x2 150 us: squares(): return lax.psum(jnp.sum(residual * residual, axis=1), ('group', 'local'))]
    ppermute x16 -> x24, waiting for transfers between devices: 216 us -> 76.7 us  [swap(): lax.ppermute(x, axis, [(i, i ^ mask) for i in range(lax.axis_size(axis))])]
    dot_general x6 -> x0, matrix products: 28.3 us -> none  [the longest x2 18.2 us: per_device(): jnp.dot(direction, kernel, precision=lax.Precision.HIGHEST)]
    pallas_call x0 -> x19, Pallas kernels: none -> 18 us  [call(): pl.pallas_call(kernel, out_shape=out_shape, in_specs=specs, out_specs=jax...]
    ppermute x16 -> x24, starting transfers between devices: 37.3 us -> 45.5 us  [swap(): lax.ppermute(x, axis, [(i, i ^ mask) for i in range(lax.axis_size(axis))])]
    dot_general x1 -> x0, local copies, waits for them, and re-layouts: 6.45 us -> none  [distant_contribution(): jnp.dot(rounded_values, flat, preferred_element_type=jnp.float32)]
    unnamed x37 -> x20, local copies, waits for them, and re-layouts: 11.1 us -> 10.3 us
  transfers between devices with their start and end apart: 16 -> 24, of which waited for: 14 -> 21; matrix products, arithmetic and copies ran while one was open for 6% -> 6% of each run, Pallas kernels for 0% -> 3%
where the time goes in v1:
time: 161 us; the launch traced here: 160 us
  waiting for transfers between devices  76.7 us (48%)
  starting transfers between devices  45.5 us (28%)
  Pallas kernels  18 us (11%)
  local copies, waits for them, and re-layouts  17.8 us (11%)
    ppermute x24, waiting for transfers between devices, swap(): lax.ppermute(x, axis, [(i, i ^ mask) for i in range(lax.axis_size(axis))])  76.7 us
    ppermute x24, starting transfers between devices, swap(): lax.ppermute(x, axis, [(i, i ^ mask) for i in range(lax.axis_size(axis))])  45.5 us
    pallas_call x19, Pallas kernels, call(): pl.pallas_call(kernel, out_shape=out_shape, in_specs=specs, out_specs=jax...  18 us
    unnamed x20, local copies, waits for them, and re-layouts  10.3 us
    gather x1, local copies, waits for them, and re-layouts, per_device(): tree_noise = jnp.take(noise, index, axis=0)[None, :]  4.53 us
  transfers between devices with their start and end apart: 24, of which 21 were waited for; matrix products, arithmetic and copies ran while one was open for 6% of the time, Pallas kernels for 3%

profile of v1, /device:TPU:1, one launch (start us, length us, event | category | flops | bytes accessed | tf_op | source)
XLA Modules:
  0.0 160.1 jit_solution(13713087768621247517)
XLA Ops:
  0.7 5.1 %copy.15 = bf16[1024,8,256]{2,0,1:T(8,128)(2,1)} copy(bf16[1024,8,256]{2,1,0:T(8,128)(2,1)} %param.10) | data formatting | bytes 8388608 | tf_op args[4]
  15.8 9.2 %collective-permute-done.1.r2.refs_2_ = f32[32,2048]{1,0:T(8,128)S(1)} collective-permute-done((f32[32,2048]{1,0:T(8,128)S(1)}, f32[32,2048]{1,0:T(8,128)S(1)}, u32[]{:S(2)}, u32[]{:S(2)}) %collective-permute-start.1) | collective-permute-done | bytes 262176 | tf_op jit(solution)/shard_map/ppermute | solution.py:199
  28.7 3.1 %collective-permute-done.3.other.refs_4_ = f32[32,1536]{1,0:T(8,128)S(1)} collective-permute-done((f32[32,1536]{1,0:T(8,128)S(1)}, f32[32,1536]{1,0:T(8,128)S(1)}, u32[]{:S(2)}, u32[]{:S(2)}) %collective-permute-start.3) | collective-permute-done | bytes 196640 | tf_op jit(solution)/shard_map/ppermute | solution.py:199
  31.8 3.1 %collective-permute-start.4 = (f32[32,1280]{1,0:T(8,128)S(1)}, f32[32,1280]{1,0:T(8,128)S(1)}, u32[]{:S(2)}, u32[]{:S(2)}) collective-permute-start(f32[32,1280]{1,0:T(8,128)S(1)} %shard_map.79.own), channel_id=1, source_target_pairs={{0,8},{1,9},{2,10},{3,11},{4,12},{5,13},{6,14},{7,15},{8,0},{9,1},... | collective-permute-start | bytes 491528 | tf_op jit(solution)/shard_map/ppermute | solution.py:199
  34.9 4.9 %collective-permute-done.4.other.refs_5_ = f32[32,1280]{1,0:T(8,128)S(1)} collective-permute-done((f32[32,1280]{1,0:T(8,128)S(1)}, f32[32,1280]{1,0:T(8,128)S(1)}, u32[]{:S(2)}, u32[]{:S(2)}) %collective-permute-start.4) | collective-permute-done | bytes 163872 | tf_op jit(solution)/shard_map/ppermute | solution.py:199
  39.8 3.2 %collective-permute-start.5 = (f32[32,1024]{1,0:T(8,128)S(1)}, f32[32,1024]{1,0:T(8,128)S(1)}, u32[]{:S(2)}, u32[]{:S(2)}) collective-permute-start(f32[32,1024]{1,0:T(8,128)S(1)} %shard_map.80.own), channel_id=1, source_target_pairs={{0,24},{1,25},{2,26},{3,27},{4,28},{5,29},{6,30},{7,31},{8,16},{9,... | collective-permute-start | bytes 393224 | tf_op jit(solution)/shard_map/ppermute | solution.py:199
  43.1 3.1 %collective-permute-done.5.other.refs_6_ = f32[32,1024]{1,0:T(8,128)S(1)} collective-permute-done((f32[32,1024]{1,0:T(8,128)S(1)}, f32[32,1024]{1,0:T(8,128)S(1)}, u32[]{:S(2)}, u32[]{:S(2)}) %collective-permute-start.5) | collective-permute-done | bytes 131104 | tf_op jit(solution)/shard_map/ppermute | solution.py:199
  46.2 4.7 %collective-permute-start.6 = (f32[32,768]{1,0:T(8,128)S(1)}, f32[32,768]{1,0:T(8,128)S(1)}, u32[]{:S(2)}, u32[]{:S(2)}) collective-permute-start(f32[32,768]{1,0:T(8,128)S(1)} %shard_map.81.own), channel_id=1, source_target_pairs={{0,32},{32,0},{64,96},{96,64},{128,160},{160,128},{192,224},{224,1... | collective-permute-start | bytes 294920 | tf_op jit(solution)/shard_map/ppermute | solution.py:199
  60.5 4.5 %gather_fusion.1 = f32[1024]{0:T(1024)S(1)} fusion(f32[1024]{0:T(1024)S(1)} %copy-done, s32[1024]{0:T(1024)S(1)} %broadcast_clamp_fusion), kind=kCustom, calls=%fused_computation.1 | custom fusion | bytes 12288 | tf_op jit(solution)/shard_map/jit(_take)/gather | solution.py:238
  69.3 5.1 %shard_map.85 = (f32[128,1024]{1,0:T(8,128)S(1)}, bf16[1024,1024]{1,0:T(8,128)(2,1)S(1)}, bf16[1024,1024]{1,0:T(8,128)(2,1)S(1)}) custom-call(f32[3,1024]{1,0:T(4,128)S(1)} %copy.13.rows_ref, f32[1024,3]{1,0:T(8,128)S(1)} %select_multiply_fusion.cols_ref, f32[1,1024]{1,0:T(1,128)S(1)} %and_select_fusion.noise_ref.refs_9_, f32[128,1024]{1,0:T(8,128)S(1)} %copy-done.2), custom_call_target="tpu_custom_call" | custom-call | flops 805306368 | bytes 1048576 | tf_op jit(solution)/shard_map/pallas_call | solution.py:31
  80.0 6.6 %shard_map.86 = (f32[32,2176]{1,0:T(8,128)S(1)}, f32[32,2176]{1,0:T(8,128)S(1)}, f32[32,2176]{1,0:T(8,128)S(1)}, f32[32,2176]{1,0:T(8,128)S(1)}, f32[128,1024]{1,0:T(8,128)S(1)}, /*index=5*/f32[128,1024]{1,0:T(8,128)S(1)}) custom-call(s32[1]{0:T(128)} %bitcast.y_ref, f32[32,2048]{1,0:T(8,128)S(1)} %get-tuple-element.27.refs_0_, ...), custom_call_target="tpu_custom_call" | custom-call | flops 1073741824 | bytes 1048576 | tf_op jit(solution)/shard_map/pallas_call | solution.py:31
  86.7 3.8 %collective-permute-start.13 = (f32[32,2176]{1,0:T(8,128)S(1)}, f32[32,2176]{1,0:T(8,128)S(1)}, u32[]{:S(2)}, u32[]{:S(2)}) collective-permute-start(f32[32,2176]{1,0:T(8,128)S(1)} %get-tuple-element.36), channel_id=1, source_target_pairs={{0,2},{1,3},{2,0},{3,1},{4,6},{5,7},{6,4},{7,5},{8,10},{9,11},{10,... | collective-permute-start | bytes 835592 | tf_op jit(solution)/shard_map/ppermute | solution.py:199
  92.7 8.3 %collective-permute-done.13.r2.refs_2_ = f32[32,2176]{1,0:T(8,128)S(1)} collective-permute-done((f32[32,2176]{1,0:T(8,128)S(1)}, f32[32,2176]{1,0:T(8,128)S(1)}, u32[]{:S(2)}, u32[]{:S(2)}) %collective-permute-start.13) | collective-permute-done | bytes 278560 | tf_op jit(solution)/shard_map/ppermute | solution.py:199
  101.0 3.4 %collective-permute-done.14.r3.refs_3_ = f32[32,2176]{1,0:T(8,128)S(1)} collective-permute-done((f32[32,2176]{1,0:T(8,128)S(1)}, f32[32,2176]{1,0:T(8,128)S(1)}, u32[]{:S(2)}, u32[]{:S(2)}) %collective-permute-start.14) | collective-permute-done | bytes 278560 | tf_op jit(solution)/shard_map/ppermute | solution.py:199
  107.1 3.2 %collective-permute-done.15.other.refs_4_ = f32[32,1664]{1,0:T(8,128)S(1)} collective-permute-done((f32[32,1664]{1,0:T(8,128)S(1)}, f32[32,1664]{1,0:T(8,128)S(1)}, u32[]{:S(2)}, u32[]{:S(2)}) %collective-permute-start.15) | collective-permute-done | bytes 213024 | tf_op jit(solution)/shard_map/ppermute | solution.py:199
  110.5 3.2 %collective-permute-start.16 = (f32[32,1408]{1,0:T(8,128)S(1)}, f32[32,1408]{1,0:T(8,128)S(1)}, u32[]{:S(2)}, u32[]{:S(2)}) collective-permute-start(f32[32,1408]{1,0:T(8,128)S(1)} %shard_map.88.own), channel_id=1, source_target_pairs={{0,8},{1,9},{2,10},{3,11},{4,12},{5,13},{6,14},{7,15},{8,0},{9,1},... | collective-permute-start | bytes 540680 | tf_op jit(solution)/shard_map/ppermute | solution.py:199
  113.7 4.8 %collective-permute-done.16.other.refs_5_ = f32[32,1408]{1,0:T(8,128)S(1)} collective-permute-done((f32[32,1408]{1,0:T(8,128)S(1)}, f32[32,1408]{1,0:T(8,128)S(1)}, u32[]{:S(2)}, u32[]{:S(2)}) %collective-permute-start.16) | collective-permute-done | bytes 180256 | tf_op jit(solution)/shard_map/ppermute | solution.py:199
  120.3 6.2 %collective-permute-done.17.other.refs_6_ = f32[32,1152]{1,0:T(8,128)S(1)} collective-permute-done((f32[32,1152]{1,0:T(8,128)S(1)}, f32[32,1152]{1,0:T(8,128)S(1)}, u32[]{:S(2)}, u32[]{:S(2)}) %collective-permute-start.17) | collective-permute-done | bytes 147488 | tf_op jit(solution)/shard_map/ppermute | solution.py:199
  126.7 4.5 %collective-permute-start.18 = (f32[32,896]{1,0:T(8,128)S(1)}, f32[32,896]{1,0:T(8,128)S(1)}, u32[]{:S(2)}, u32[]{:S(2)}) collective-permute-start(f32[32,896]{1,0:T(8,128)S(1)} %shard_map.90.own), channel_id=1, source_target_pairs={{0,32},{32,0},{64,96},{96,64},{128,160},{160,128},{192,224},{224,1... | collective-permute-start | bytes 344072 | tf_op jit(solution)/shard_map/ppermute | solution.py:199
  132.2 3.7 %collective-permute-done.19.other.refs_8_ = f32[32,640]{1,0:T(8,128)S(1)} collective-permute-done((f32[32,640]{1,0:T(8,128)S(1)}, f32[32,640]{1,0:T(8,128)S(1)}, u32[]{:S(2)}, u32[]{:S(2)}) %collective-permute-start.19) | collective-permute-done | bytes 81952 | tf_op jit(solution)/shard_map/ppermute | solution.py:199
  136.2 3.9 %collective-permute-done.20.other.refs_9_ = f32[32,384]{1,0:T(8,128)S(1)} collective-permute-done((f32[32,384]{1,0:T(8,128)S(1)}, f32[32,384]{1,0:T(8,128)S(1)}, u32[]{:S(2)}, u32[]{:S(2)}) %collective-permute-start.20) | collective-permute-done | bytes 49184 | tf_op jit(solution)/shard_map/ppermute | solution.py:199
  146.2 5.7 %collective-permute-done.22.refs_2_ = f32[32,2176]{1,0:T(8,128)S(1)} collective-permute-done((f32[32,2176]{1,0:T(8,128)S(1)}, f32[32,2176]{1,0:T(8,128)S(1)}, u32[]{:S(2)}, u32[]{:S(2)}) %collective-permute-start.22) | collective-permute-done | bytes 278560 | tf_op jit(solution)/shard_map/ppermute | solution.py:199
  152.0 3.6 %collective-permute-done.23.refs_3_ = f32[32,2176]{1,0:T(8,128)S(1)} collective-permute-done((f32[32,2176]{1,0:T(8,128)S(1)}, f32[32,2176]{1,0:T(8,128)S(1)}, u32[]{:S(2)}, u32[]{:S(2)}) %collective-permute-start.23) | collective-permute-done | bytes 278560 | tf_op jit(solution)/shard_map/ppermute | solution.py:199
  155.5 4.6 %shard_map.95 = (f32[128,1024]{1,0:T(8,128)}, f32[128,1024]{1,0:T(8,128)}) custom-call(s32[1]{0:T(128)} %bitcast.y_ref, f32[32,2176]{1,0:T(8,128)S(1)} %get-tuple-element.38.refs_0_, f32[32,2176]{1,0:T(8,128)S(1)} %collective-permute-done.21.refs_1_, f32[32,2176]{1,0:T(8,128)S(1)} %collective-permute-done.22.refs_2_, ...), custom_call_target="tpu_custom_call" | custom-call | flops 536870912 | bytes 1048576 | tf_op jit(solution)/shard_map/pallas_call | solution.py:31
  (72 shorter events, 47.7 us)
Async XLA Ops:
  8.7 7.0 %collective-permute-start = (f32[32,2048]{1,0:T(8,128)S(1)}, f32[32,2048]{1,0:T(8,128)S(1)}, u32[]{:S(2)}, u32[]{:S(2)}) collective-permute-start(f32[32,2048]{1,0:T(8,128)S(1)} %get-tuple-element.24), channel_id=1, source_target_pairs={{0,1},{1,0},{2,3},{3,2},{4,5},{5,4},{6,7},{7,6},{8,9},{9,8},{10,11... | collective-permute-start | bytes 786440 | tf_op jit(solution)/shard_map/ppermute | solution.py:199
  11.0 14.0 %collective-permute-start.1 = (f32[32,2048]{1,0:T(8,128)S(1)}, f32[32,2048]{1,0:T(8,128)S(1)}, u32[]{:S(2)}, u32[]{:S(2)}) collective-permute-start(f32[32,2048]{1,0:T(8,128)S(1)} %get-tuple-element.25), channel_id=1, source_target_pairs={{0,2},{1,3},{2,0},{3,1},{4,6},{5,7},{6,4},{7,5},{8,10},{9,11},{10,... | collective-permute-start | bytes 786440 | tf_op jit(solution)/shard_map/ppermute | solution.py:199
  13.6 13.4 %collective-permute-start.2 = (f32[32,2048]{1,0:T(8,128)S(1)}, f32[32,2048]{1,0:T(8,128)S(1)}, u32[]{:S(2)}, u32[]{:S(2)}) collective-permute-start(f32[32,2048]{1,0:T(8,128)S(1)} %get-tuple-element.26), channel_id=1, source_target_pairs={{0,3},{1,2},{2,1},{3,0},{4,7},{5,6},{6,5},{7,4},{8,11},{9,10},{10,... | collective-permute-start | bytes 786440 | tf_op jit(solution)/shard_map/ppermute | solution.py:199
  27.0 4.8 %collective-permute-start.3 = (f32[32,1536]{1,0:T(8,128)S(1)}, f32[32,1536]{1,0:T(8,128)S(1)}, u32[]{:S(2)}, u32[]{:S(2)}) collective-permute-start(f32[32,1536]{1,0:T(8,128)S(1)} %shard_map.78.own), channel_id=1, source_target_pairs={{0,4},{1,5},{2,6},{3,7},{4,0},{5,1},{6,2},{7,3},{8,12},{9,13},{10,... | collective-permute-start | bytes 589832 | tf_op jit(solution)/shard_map/ppermute | solution.py:199
  31.8 8.0 %collective-permute-start.4 = (f32[32,1280]{1,0:T(8,128)S(1)}, f32[32,1280]{1,0:T(8,128)S(1)}, u32[]{:S(2)}, u32[]{:S(2)}) collective-permute-start(f32[32,1280]{1,0:T(8,128)S(1)} %shard_map.79.own), channel_id=1, source_target_pairs={{0,8},{1,9},{2,10},{3,11},{4,12},{5,13},{6,14},{7,15},{8,0},{9,1},... | collective-permute-start | bytes 491528 | tf_op jit(solution)/shard_map/ppermute | solution.py:199
  39.8 6.3 %collective-permute-start.5 = (f32[32,1024]{1,0:T(8,128)S(1)}, f32[32,1024]{1,0:T(8,128)S(1)}, u32[]{:S(2)}, u32[]{:S(2)}) collective-permute-start(f32[32,1024]{1,0:T(8,128)S(1)} %shard_map.80.own), channel_id=1, source_target_pairs={{0,24},{1,25},{2,26},{3,27},{4,28},{5,29},{6,30},{7,31},{8,16},{9,... | collective-permute-start | bytes 393224 | tf_op jit(solution)/shard_map/ppermute | solution.py:199
  46.2 7.8 %collective-permute-start.6 = (f32[32,768]{1,0:T(8,128)S(1)}, f32[32,768]{1,0:T(8,128)S(1)}, u32[]{:S(2)}, u32[]{:S(2)}) collective-permute-start(f32[32,768]{1,0:T(8,128)S(1)} %shard_map.81.own), channel_id=1, source_target_pairs={{0,32},{32,0},{64,96},{96,64},{128,160},{160,128},{192,224},{224,1... | collective-permute-start | bytes 294920 | tf_op jit(solution)/shard_map/ppermute | solution.py:199
  54.0 3.8 %collective-permute-start.7 = (f32[32,512]{1,0:T(8,128)S(1)}, f32[32,512]{1,0:T(8,128)S(1)}, u32[]{:S(2)}, u32[]{:S(2)}) collective-permute-start(f32[32,512]{1,0:T(8,128)S(1)} %shard_map.82.own), channel_id=1, source_target_pairs={{0,64},{32,96},{64,0},{96,32},{128,192},{160,224},{192,128},{224,1... | collective-permute-start | bytes 196616 | tf_op jit(solution)/shard_map/ppermute | solution.py:199
  57.8 7.4 %collective-permute-start.8 = (f32[32,256]{1,0:T(8,128)S(1)}, f32[32,256]{1,0:T(8,128)S(1)}, u32[]{:S(2)}, u32[]{:S(2)}) collective-permute-start(f32[32,256]{1,0:T(8,128)S(1)} %shard_map.83), channel_id=1, source_target_pairs={{0,192},{32,224},{64,128},{96,160},{128,64},{160,96},{192,0},{224,... | collective-permute-start | bytes 98312 | tf_op jit(solution)/shard_map/ppermute | solution.py:199
  65.3 11.9 %collective-permute-start.9 = (f32[32,2048]{1,0:T(8,128)S(1)}, f32[32,2048]{1,0:T(8,128)S(1)}, u32[]{:S(2)}, u32[]{:S(2)}) collective-permute-start(f32[32,2048]{1,0:T(8,128)S(1)} %get-tuple-element.28), channel_id=1, source_target_pairs={{0,1},{1,0},{2,3},{3,2},{4,5},{5,4},{6,7},{7,6},{8,9},{9,8},{10,11... | collective-permute-start | bytes 786440 | tf_op jit(solution)/shard_map/ppermute | solution.py:199
  65.4 12.1 %collective-permute-start.10 = (f32[32,2048]{1,0:T(8,128)S(1)}, f32[32,2048]{1,0:T(8,128)S(1)}, u32[]{:S(2)}, u32[]{:S(2)}) collective-permute-start(f32[32,2048]{1,0:T(8,128)S(1)} %get-tuple-element.29), channel_id=1, source_target_pairs={{0,2},{1,3},{2,0},{3,1},{4,6},{5,7},{6,4},{7,5},{8,10},{9,11},{10,... | collective-permute-start | bytes 786440 | tf_op jit(solution)/shard_map/ppermute | solution.py:199
  66.6 13.4 %collective-permute-start.11 = (f32[32,2048]{1,0:T(8,128)S(1)}, f32[32,2048]{1,0:T(8,128)S(1)}, u32[]{:S(2)}, u32[]{:S(2)}) collective-permute-start(f32[32,2048]{1,0:T(8,128)S(1)} %get-tuple-element.30), channel_id=1, source_target_pairs={{0,3},{1,2},{2,1},{3,0},{4,7},{5,6},{6,5},{7,4},{8,11},{9,10},{10,... | collective-permute-start | bytes 786440 | tf_op jit(solution)/shard_map/ppermute | solution.py:199
  86.6 6.1 %collective-permute-start.12 = (f32[32,2176]{1,0:T(8,128)S(1)}, f32[32,2176]{1,0:T(8,128)S(1)}, u32[]{:S(2)}, u32[]{:S(2)}) collective-permute-start(f32[32,2176]{1,0:T(8,128)S(1)} %get-tuple-element.35), channel_id=1, source_target_pairs={{0,1},{1,0},{2,3},{3,2},{4,5},{5,4},{6,7},{7,6},{8,9},{9,8},{10,11... | collective-permute-start | bytes 835592 | tf_op jit(solution)/shard_map/ppermute | solution.py:199
  86.7 14.2 %collective-permute-start.13 = (f32[32,2176]{1,0:T(8,128)S(1)}, f32[32,2176]{1,0:T(8,128)S(1)}, u32[]{:S(2)}, u32[]{:S(2)}) collective-permute-start(f32[32,2176]{1,0:T(8,128)S(1)} %get-tuple-element.36), channel_id=1, source_target_pairs={{0,2},{1,3},{2,0},{3,1},{4,6},{5,7},{6,4},{7,5},{8,10},{9,11},{10,... | collective-permute-start | bytes 835592 | tf_op jit(solution)/shard_map/ppermute | solution.py:199
  90.5 13.9 %collective-permute-start.14 = (f32[32,2176]{1,0:T(8,128)S(1)}, f32[32,2176]{1,0:T(8,128)S(1)}, u32[]{:S(2)}, u32[]{:S(2)}) collective-permute-start(f32[32,2176]{1,0:T(8,128)S(1)} %get-tuple-element.37), channel_id=1, source_target_pairs={{0,3},{1,2},{2,1},{3,0},{4,7},{5,6},{6,5},{7,4},{8,11},{9,10},{10,... | collective-permute-start | bytes 835592 | tf_op jit(solution)/shard_map/ppermute | solution.py:199
  104.5 5.9 %collective-permute-start.15 = (f32[32,1664]{1,0:T(8,128)S(1)}, f32[32,1664]{1,0:T(8,128)S(1)}, u32[]{:S(2)}, u32[]{:S(2)}) collective-permute-start(f32[32,1664]{1,0:T(8,128)S(1)} %shard_map.87.own), channel_id=1, source_target_pairs={{0,4},{1,5},{2,6},{3,7},{4,0},{5,1},{6,2},{7,3},{8,12},{9,13},{10,... | collective-permute-start | bytes 638984 | tf_op jit(solution)/shard_map/ppermute | solution.py:199
  110.5 8.0 %collective-permute-start.16 = (f32[32,1408]{1,0:T(8,128)S(1)}, f32[32,1408]{1,0:T(8,128)S(1)}, u32[]{:S(2)}, u32[]{:S(2)}) collective-permute-start(f32[32,1408]{1,0:T(8,128)S(1)} %shard_map.88.own), channel_id=1, source_target_pairs={{0,8},{1,9},{2,10},{3,11},{4,12},{5,13},{6,14},{7,15},{8,0},{9,1},... | collective-permute-start | bytes 540680 | tf_op jit(solution)/shard_map/ppermute | solution.py:199
  118.6 8.0 %collective-permute-start.17 = (f32[32,1152]{1,0:T(8,128)S(1)}, f32[32,1152]{1,0:T(8,128)S(1)}, u32[]{:S(2)}, u32[]{:S(2)}) collective-permute-start(f32[32,1152]{1,0:T(8,128)S(1)} %shard_map.89.own), channel_id=1, source_target_pairs={{0,24},{1,25},{2,26},{3,27},{4,28},{5,29},{6,30},{7,31},{8,16},{9,... | collective-permute-start | bytes 442376 | tf_op jit(solution)/shard_map/ppermute | solution.py:199
  126.7 5.4 %collective-permute-start.18 = (f32[32,896]{1,0:T(8,128)S(1)}, f32[32,896]{1,0:T(8,128)S(1)}, u32[]{:S(2)}, u32[]{:S(2)}) collective-permute-start(f32[32,896]{1,0:T(8,128)S(1)} %shard_map.90.own), channel_id=1, source_target_pairs={{0,32},{32,0},{64,96},{96,64},{128,160},{160,128},{192,224},{224,1... | collective-permute-start | bytes 344072 | tf_op jit(solution)/shard_map/ppermute | solution.py:199
  132.2 3.7 %collective-permute-start.19 = (f32[32,640]{1,0:T(8,128)S(1)}, f32[32,640]{1,0:T(8,128)S(1)}, u32[]{:S(2)}, u32[]{:S(2)}) collective-permute-start(f32[32,640]{1,0:T(8,128)S(1)} %shard_map.91.own), channel_id=1, source_target_pairs={{0,64},{32,96},{64,0},{96,32},{128,192},{160,224},{192,128},{224,1... | collective-permute-start | bytes 245768 | tf_op jit(solution)/shard_map/ppermute | solution.py:199
  136.0 4.2 %collective-permute-start.20 = (f32[32,384]{1,0:T(8,128)S(1)}, f32[32,384]{1,0:T(8,128)S(1)}, u32[]{:S(2)}, u32[]{:S(2)}) collective-permute-start(f32[32,384]{1,0:T(8,128)S(1)} %shard_map.92.own), channel_id=1, source_target_pairs={{0,192},{32,224},{64,128},{96,160},{128,64},{160,96},{192,0},{224,... | collective-permute-start | bytes 147464 | tf_op jit(solution)/shard_map/ppermute | solution.py:199
  140.3 5.9 %collective-permute-start.21 = (f32[32,2176]{1,0:T(8,128)S(1)}, f32[32,2176]{1,0:T(8,128)S(1)}, u32[]{:S(2)}, u32[]{:S(2)}) collective-permute-start(f32[32,2176]{1,0:T(8,128)S(1)} %get-tuple-element.39), channel_id=1, source_target_pairs={{0,1},{1,0},{2,3},{3,2},{4,5},{5,4},{6,7},{7,6},{8,9},{9,8},{10,11... | collective-permute-start | bytes 835592 | tf_op jit(solution)/shard_map/ppermute | solution.py:199
  140.4 11.5 %collective-permute-start.22 = (f32[32,2176]{1,0:T(8,128)S(1)}, f32[32,2176]{1,0:T(8,128)S(1)}, u32[]{:S(2)}, u32[]{:S(2)}) collective-permute-start(f32[32,2176]{1,0:T(8,128)S(1)} %get-tuple-element.40), channel_id=1, source_target_pairs={{0,2},{1,3},{2,0},{3,1},{4,6},{5,7},{6,4},{7,5},{8,10},{9,11},{10,... | collective-permute-start | bytes 835592 | tf_op jit(solution)/shard_map/ppermute | solution.py:199
  141.6 13.9 %collective-permute-start.23 = (f32[32,2176]{1,0:T(8,128)S(1)}, f32[32,2176]{1,0:T(8,128)S(1)}, u32[]{:S(2)}, u32[]{:S(2)}) collective-permute-start(f32[32,2176]{1,0:T(8,128)S(1)} %get-tuple-element.41), channel_id=1, source_target_pairs={{0,3},{1,2},{2,1},{3,0},{4,7},{5,6},{6,5},{7,4},{8,11},{9,10},{10,... | collective-permute-start | bytes 835592 | tf_op jit(solution)/shard_map/ppermute | solution.py:199
  (9 other events, 203.3 us)
